TPU v7x, 32 devices: a whole 2x2x4 slice. The times are simulated.
32 devices in a mesh: scen: 2 (over y), tm: 8 (over z, x), panel: 2 (over core).
Axes of the slice: x: 2, y: 2, z: 4, core: 2. Of those that a mesh axis runs over, the one named last changes fastest.
Arguments:
- panels: bfloat16 [16, 1024, 2048], P(('scen', 'tm'), 'panel'), parts along dimension 0, may hold values from -0.1875 to 0.1875
- barrier: bfloat16 [16, 1024], P(('scen', 'tm'), 'panel'), parts along dimension 0, may hold values from 0.099609375 to 10
- counts: int32 [16, 2], P(('scen', 'tm'), 'panel'), parts along dimension 0, may hold values from 1 to 8
Outputs:
- diag_blocks: bfloat16 [16, 1024, 1024], P(('scen', 'tm'), 'panel'), parts along dimension 0
- cross_blocks: bfloat16 [16, 1024, 1024], P(('scen', 'tm'), 'panel'), parts along dimension 0
There are 2 independent parts, one for each index of `scen`. A program takes and returns all parts, laid end to end along the dimension named above; each array names one. Nothing has to cross between parts.
Inputs may be any that keep to these rules, and one draw needn't show every extreme that they name: The first 64 * counts[t, p] rows of group p of block t are live; every device of the panel axis has at least one live slot.
All inputs are finite; a program needn't handle non-finite values.
Results may differ from a plain program's by a relative error of at most 0.0059.
Values may be sent and summed in bfloat16 or wider, within the bound.
A program may use at most 64 MiB of HBM per device.

v0:
```python
from functools import partial

import jax
import jax.numpy as jnp
from jax import lax
from jax.sharding import PartitionSpec as P

PR = 64
SLOTS = 8


def passed_along(value, axis, by):
    devices = lax.axis_size(axis)
    pairs = [(i, i + by) for i in range(devices) if 0 <= i + by < devices]
    return lax.ppermute(value, axis, pairs)


def prefix_gram(row_count, left_part, right_part):
    if row_count == 0:
        return jnp.zeros((left_part.shape[1], right_part.shape[1]), jnp.float32)
    return lax.dot_general(
        left_part[:row_count],
        right_part[:row_count],
        (((0,), (0,)), ((), ())),
        preferred_element_type=jnp.float32,
    )


def live_gram(left_part, right_part, live_count):
    branches = [partial(prefix_gram, slot * PR) for slot in range(SLOTS + 1)]
    return lax.switch(live_count, branches, left_part, right_part)


def scale_rows(plain_rows, diagonal):
    return (plain_rows.astype(jnp.float32) * diagonal.astype(jnp.float32)[:, None]).astype(
        jnp.bfloat16
    )


def body(panels, barrier, counts):
    own_rows = panels[0]
    own_diag = barrier[0]
    live_count = counts[0, 0]
    states = own_rows.shape[1] // 2
    scaled = scale_rows(own_rows, own_diag)
    left_cross = live_gram(scaled[:, :states], own_rows, live_count)
    right_round = live_gram(scaled[:, states:], own_rows[:, states:], live_count).astype(
        jnp.bfloat16
    )
    came_right = passed_along(right_round, "tm", 1)
    partial_diag = (left_cross[:, :states] + came_right.astype(jnp.float32)).astype(jnp.bfloat16)
    cross_round = left_cross[:, states:].astype(jnp.bfloat16)
    diag_term = partial_diag.astype(jnp.float32)
    cross_term = cross_round.astype(jnp.float32)
    diag_total, cross_total = (
        lax.psum(diag_term.astype(jnp.bfloat16), "panel").astype(jnp.float32),
        lax.psum(cross_term.astype(jnp.bfloat16), "panel").astype(jnp.float32),
    )
    share_rows = states // lax.axis_size("panel")
    first_row = lax.axis_index("panel") * share_rows
    diag_sum = lax.dynamic_slice_in_dim(diag_total, first_row, share_rows, 0)
    cross_sum = lax.dynamic_slice_in_dim(cross_total, first_row, share_rows, 0)
    return (diag_sum.astype(jnp.bfloat16)[None], cross_sum.astype(jnp.bfloat16)[None])


def solution(mesh):
    return jax.shard_map(
        body,
        mesh=mesh,
        in_specs=(
            P(("scen", "tm"), "panel", None),
            P(("scen", "tm"), "panel"),
            P(("scen", "tm"), "panel"),
        ),
        out_specs=(P(("scen", "tm"), "panel", None), P(("scen", "tm"), "panel", None)),
        check_vma=False,
    )
```

profile of v0, /device:TPU:9, one launch (start us, length us, event | category | flops | bytes accessed | tf_op | source)
XLA Modules:
  0.0 110.9 jit_solution(17782118386800039607)
XLA Ops:
  7.2 0.0 all-reduce.3.cloned.1.call-start
  7.2 0.7 convert_element_type.53
  8.5 0.0 copy-start
  8.6 3.5 %multiply_convert_fusion = bf16[512,2048]{1,0:T(8,128)(2,1)} fusion(f32[512]{0:T(512)S(1)} %bitcast.25, bf16[1,512,2048]{2,1,0:T(8,128)(2,1)} %param.21), kind=kLoop, calls=%fused_computation.50 | loop fusion | flops 3145728 | bytes 4196352 | tf_op jit(solution)/shard_map/convert_element_type | solution.py:35
  12.1 0.0 copy-done
  12.1 3.8 %conditional.3 = (bf16[1024,1024]{1,0:T(8,128)(2,1)}) conditional(s32[]{:T(128)} %bitcast, () %tuple.64, (bf16[512,2048]{1,0:T(8,128)(2,1)}, bf16[512,2048]{1,0:T(8,128)(2,1)S(1)}) %tuple.88, (bf16[512,2048]{1,0:T(8,128)(2,1)}, bf16[512,2048]{1,0:T(8,128)(2,1)S(1)}) %tuple.89, (bf16[512,2048]{1,0:T(8,128)(2,1)}, ...), branch_computations={%region_9.0_spmd, %region_10.0_spmd, %region_11.0_spmd, %region_12... | conditional | flops 1073741824 | bytes 4194312 | solution.py:31
  12.1 3.7 %fusion.38 = bf16[1024,1024]{1,0:T(8,128)(2,1)} fusion(bf16[512,2048]{1,0:T(8,128)(2,1)S(1)} %get-tuple-element.135, bf16[512,2048]{1,0:T(8,128)(2,1)} %get-tuple-element.134), kind=kOutput, calls=%fused_computation.38 | convolution fusion | flops 805306368 | bytes 3670016 | tf_op jit(solution)/shard_map/cond/branch_6_fun/dot_general | solution.py:21
  15.9 3.1 %collective-permute-start = (bf16[1024,1024]{1,0:T(8,128)(2,1)}, bf16[1024,1024]{1,0:T(8,128)(2,1)}, u32[]{:S(2)}, u32[]{:S(2)}) collective-permute-start(bf16[1024,1024]{1,0:T(8,128)(2,1)} %get-tuple-element.149), channel_id=1, source_target_pairs={{0,2},{2,4},{4,6},{6,8},{8,10},{10,12},{12,14},{1,3},{3,5},{5,7},{... | collective-permute-start | bytes 6291464 | tf_op jit(solution)/shard_map/ppermute | solution.py:15
  18.9 7.0 %conditional.2 = (f32[1024,2048]{1,0:T(8,128)}) conditional(s32[]{:T(128)} %bitcast, () %tuple.62, (bf16[512,2048]{1,0:T(8,128)(2,1)}, bf16[512,2048]{1,0:T(8,128)(2,1)S(1)}) %tuple.96, (bf16[512,2048]{1,0:T(8,128)(2,1)}, bf16[512,2048]{1,0:T(8,128)(2,1)S(1)}) %tuple.97, (bf16[512,2048]{1,0:T(8,128)(2,1)}, ...), branch_computations={%region_0.0_spmd, %region_1.0_spmd, %region_2.0_spmd, %region_3.0_... | conditional | flops 2147483648 | bytes 11534344 | solution.py:31
  19.2 6.8 %fusion.15 = f32[1024,2048]{1,0:T(8,128)} fusion(bf16[512,2048]{1,0:T(8,128)(2,1)S(1)} %get-tuple-element.119, bf16[512,2048]{1,0:T(8,128)(2,1)} %get-tuple-element.118), kind=kOutput, calls=%fused_computation.15 | convolution fusion | flops 1610612736 | bytes 10747904 | tf_op jit(solution)/shard_map/cond/branch_6_fun/dot_general | solution.py:21
  26.0 3.9 %slice.215 = bf16[1024,1024]{1,0:T(8,128)(2,1)} slice(f32[1024,2048]{1,0:T(8,128)} %get-tuple-element.148), slice={[0:1024], [1024:2048]} | slice | bytes 4194304 | tf_op jit(solution)/shard_map/slice | solution.py:52
  29.9 35.6 %collective-permute-done = bf16[1024,1024]{1,0:T(8,128)(2,1)} collective-permute-done((bf16[1024,1024]{1,0:T(8,128)(2,1)}, bf16[1024,1024]{1,0:T(8,128)(2,1)}, u32[]{:S(2)}, u32[]{:S(2)}) %collective-permute-start) | collective-permute-done | bytes 2097184 | tf_op jit(solution)/shard_map/ppermute | solution.py:15
  65.4 5.0 %fusion.47 = bf16[1024,1024]{1,0:T(8,128)(2,1)} fusion(f32[1024,2048]{1,0:T(8,128)} %get-tuple-element.148, bf16[1024,1024]{1,0:T(8,128)(2,1)} %collective-permute-done), kind=kLoop, calls=%fused_computation.49 | loop fusion | flops 3145728 | bytes 8388608 | tf_op jit(solution)/shard_map/convert_element_type | solution.py:51
  70.4 0.0 all-reduce.3.cloned.1.call-update
  70.4 30.6 %all-reduce.3.cloned.1.call-done = (bf16[1024,1024]{1,0:T(8,128)(2,1)}, bf16[1024,1024]{1,0:T(8,128)(2,1)}) async-done(((bf16[1024,1024]{1,0:T(8,128)(2,1)}, bf16[1024,1024]{1,0:T(8,128)(2,1)}), (bf16[1024,1024]{1,0:T(8,128)(2,1)}, bf16[1024,1024]{1,0:T(8,128)(2,1)})) %all-reduce.3.cloned.1.call-update) | async-done | bytes 4194320 | tf_op jit(solution)/shard_map/psum | solution.py:56
  101.0 3.0 %fusion.48 = (bf16[1,512,1024]{2,1,0:T(8,128)(2,1)}, bf16[1,512,1024]{2,1,0:T(8,128)(2,1)}) fusion(bf16[1024,1024]{1,0:T(8,128)(2,1)} %get-tuple-element.142, s32[]{:T(128)S(6)} %select_n.4, bf16[1024,1024]{1,0:T(8,128)(2,1)} %get-tuple-element.143), kind=kLoop, calls=%fused_computation.53 | loop fusion | flops 2097152 | bytes 4194308 | tf_op jit(solution)/shard_map/broadcast_in_dim | solution.py:63
Async XLA Ops:
  7.2 93.9 %all-reduce.3.cloned.1.call-start = ((), (), s32[]{:S(2)}) async-start(), calls=%async_computation | async-start | bytes 8388608 | tf_op jit(solution)/shard_map/psum | solution.py:56
  8.5 3.6 %copy-start = (bf16[1,512,2048]{2,1,0:T(8,128)(2,1)S(1)}, bf16[1,512,2048]{2,1,0:T(8,128)(2,1)}, u32[]{:S(2)}) copy-start(bf16[1,512,2048]{2,1,0:T(8,128)(2,1)} %param.21) | copy-start | bytes 6291460
  15.9 49.6 %collective-permute-start = (bf16[1024,1024]{1,0:T(8,128)(2,1)}, bf16[1024,1024]{1,0:T(8,128)(2,1)}, u32[]{:S(2)}, u32[]{:S(2)}) collective-permute-start(bf16[1024,1024]{1,0:T(8,128)(2,1)} %get-tuple-element.149), channel_id=1, source_target_pairs={{0,2},{2,4},{4,6},{6,8},{8,10},{10,12},{12,14},{1,3},{3,5},{5,7},{... | collective-permute-start | bytes 6291464 | tf_op jit(solution)/shard_map/ppermute | solution.py:15
Sparse Core Ops, SparseCore 0:
  70.6 30.4 all-reduce.2
where the time goes:
time: 112 us; the launch traced here: 111 us
  waiting for transfers between devices  66.2 us (59%)
  between operations  14.7 us (13%)
  other arithmetic  12.2 us (11%)
  matrix products  10.5 us (9%)
  local copies, waits for them, and re-layouts  3.92 us (4%)
  starting transfers between devices  3.1 us (3%)
    ppermute x1, waiting for transfers between devices, passed_along(): return lax.ppermute(value, axis, pairs)  35.6 us
    psum x1, waiting for transfers between devices, body(): lax.psum(diag_term.astype(jnp.bfloat16), 'panel').astype(jnp.float32)  30.6 us
    dot_general x2, matrix products, prefix_gram(): lax.dot_general(left_part[:row_count], right_part[:row_count], (((0,), (0...  10.5 us
    convert_element_type x1, other arithmetic, body(): (left_cross[:, :states] + came_right.astype(jnp.float32)).astype(jnp.bflo...  4.97 us
    slice x1, local copies, waits for them, and re-layouts, body(): cross_round = left_cross[:, states:].astype(jnp.bfloat16)  3.91 us
    convert_element_type x1, other arithmetic, scale_rows(): (plain_rows.astype(jnp.float32) * diagonal.astype(jnp.float32)[:, None])....  3.54 us
    ppermute x1, starting transfers between devices, passed_along(): return lax.ppermute(value, axis, pairs)  3.06 us
    broadcast_in_dim x1, other arithmetic, body(): diag_sum.astype(jnp.bfloat16)[None]  3.03 us
  transfers between devices with their start and end apart: 2, of which 2 were waited for; matrix products, arithmetic and copies ran while one was open for 10% of the time, Pallas kernels for 0%

commit v1 on v0

v1 whole, which is shorter than its diff:
```python
import functools

import jax
import jax.numpy as jnp
from jax import lax
from jax.experimental import pallas as pl
from jax.experimental.pallas import tpu as pltpu
from jax.sharding import PartitionSpec as P

PR = 64
MESH = pl.DeviceIdType.MESH
F32 = jnp.float32
BF16 = jnp.bfloat16
PAD = 16


def gram(left, right):
    return jnp.dot(left, right, preferred_element_type=F32)


def kernel(
    blocks,
    panels_ref,
    barrier_ref,
    counts_ref,
    diag_ref,
    cross_ref,
    rows,
    weight_row,
    weight_peer,
    weight_col,
    right_t,
    left_t,
    total,
    out_tiles,
    in_tiles,
    peer_tiles,
    local_sem,
    peer_send,
    peer_recv,
    link_send,
    link_recv,
    pass_send,
    pass_recv,
):
    R = panels_ref.shape[1]
    B = panels_ref.shape[2] // 2
    H = B // 2
    Q = H // 2
    s, t, p = lax.axis_index("scen"), lax.axis_index("tm"), lax.axis_index("panel")
    q = 1 - p
    peer = (s, t, q)
    after = (s, lax.rem(t + 1, blocks), p)
    before = (s, lax.rem(t + blocks - 1, blocks), p)
    has_before, has_after = t > 0, t < blocks - 1

    local_right = pltpu.make_async_copy(
        panels_ref.at[0, :, pl.ds(B, B)], rows.at[pl.ds(0, R), pl.ds(B, B)], local_sem.at[0]
    )
    local_left = pltpu.make_async_copy(
        panels_ref.at[0, :, pl.ds(0, B)], rows.at[pl.ds(0, R), pl.ds(0, B)], local_sem.at[1]
    )
    local_right.start()
    local_left.start()

    entry = pltpu.get_barrier_semaphore()
    pl.semaphore_signal(entry, inc=1, device_id=peer, device_id_type=MESH)

    @pl.when(has_before)
    def _():
        pl.semaphore_signal(entry, inc=1, device_id=before, device_id_type=MESH)

    @pl.when(has_after)
    def _():
        pl.semaphore_signal(entry, inc=1, device_id=after, device_id_type=MESH)

    spot = lax.broadcasted_iota(jnp.int32, (8, R), 1)
    diagonal = jnp.broadcast_to(barrier_ref[...].astype(F32), (8, R))
    weight_row[...] = jnp.where(spot < counts_ref[0, 0] * PR, diagonal, 0.0)

    def right_tile(half, tile):
        return pl.ds(pl.multiple_of(B + half * H + tile * Q, Q), Q)

    def to_peer(columns, which):
        return pltpu.make_async_remote_copy(
            src_ref=panels_ref.at[0, :, columns],
            dst_ref=rows.at[pl.ds(R, R), columns],
            send_sem=peer_send.at[which],
            recv_sem=peer_recv.at[which],
            device_id=peer,
            device_id_type=MESH,
        )

    def exchange(dest):
        rest = 1 - dest
        return [
            to_peer(right_tile(dest, 0), 0),
            to_peer(right_tile(rest, dest), 1),
            to_peer(right_tile(dest, 1), 2),
            to_peer(right_tile(rest, 1 - dest), 3),
            to_peer(pl.ds(pl.multiple_of(dest * H, H), H), 4),
            to_peer(pl.ds(pl.multiple_of(rest * H, H), H), 5),
        ]

    weight_copy = pltpu.make_async_remote_copy(
        src_ref=weight_row,
        dst_ref=weight_peer,
        send_sem=peer_send.at[6],
        recv_sem=peer_recv.at[6],
        device_id=peer,
        device_id_type=MESH,
    )
    pl.semaphore_wait(entry, 1 + has_before.astype(jnp.int32) + has_after.astype(jnp.int32))
    weight_copy.start()
    sent = exchange(q)
    came = exchange(p)
    for copy in sent:
        copy.start()

    def spread(row):
        return jnp.broadcast_to(row[0:1, :], (128, R)).T

    def scaled_t(group, columns, width):
        weight = weight_col[pl.ds(group * R, R), :]
        plain = rows[pl.ds(group * R, R), columns].astype(F32)
        weight = jnp.concatenate([weight] * (width // 128), axis=1)
        return (plain * weight).astype(BF16).T

    weight_col[pl.ds(0, R), :] = spread(weight_row[...])
    local_right.wait()
    for tile in range(2):
        right_t[pl.ds(tile * Q, Q), pl.ds(0, R)] = scaled_t(0, right_tile(p, tile), Q)
    weight_copy.wait_recv()
    weight_col[pl.ds(R, R), :] = spread(weight_peer[...])

    def link(first, length, which):
        return pltpu.make_async_remote_copy(
            src_ref=out_tiles.at[pl.ds(first, length), :],
            dst_ref=in_tiles.at[pl.ds(first, length), :],
            send_sem=link_send.at[which],
            recv_sem=link_recv.at[which],
            device_id=after,
            device_id_type=MESH,
        )

    links = [link(0, Q, 0), link(Q, Q, 1), link(2 * Q, Q, 2), link(3 * Q, Q + PAD, 3)]

    def send_on(which):
        @pl.when(has_after)
        def _():
            links[which].start()

    lower = lax.broadcasted_iota(jnp.int32, (Q, Q), 0)
    upper = lax.broadcasted_iota(jnp.int32, (Q, Q), 1)

    for tile in range(2):
        came[2 * tile].wait_recv()
        right_t[pl.ds(tile * Q, Q), pl.ds(R, R)] = scaled_t(1, right_tile(p, tile), Q)
        came[2 * tile + 1].wait_recv()
        other = lax.rem(tile + p, 2)
        out_tiles[pl.ds(tile * Q, Q), :] = gram(
            right_t[pl.ds(tile * Q, Q), :], rows[:, right_tile(q, other)]
        ).astype(BF16)
        send_on(tile)
    out_tiles[pl.ds(2 * Q, Q), :] = gram(
        right_t[pl.ds(0, Q), :], rows[:, right_tile(p, 1)]
    ).astype(BF16)
    send_on(2)
    first = gram(right_t[pl.ds(0, Q), :], rows[:, right_tile(p, 0)])
    second = gram(right_t[pl.ds(Q, Q), :], rows[:, right_tile(p, 1)])
    out_tiles[pl.ds(3 * Q, Q), :] = jnp.where(upper >= lower, first, second).astype(BF16)
    middle = jnp.sum(jnp.where(upper == lower, second, 0.0), axis=0, keepdims=True)
    out_tiles[pl.ds(4 * Q, PAD), :] = jnp.broadcast_to(middle, (PAD, Q)).astype(BF16)
    send_on(3)

    own_left = pl.ds(pl.multiple_of(p * H, H), H)
    local_left.wait()
    left_t[:, pl.ds(0, R)] = scaled_t(0, own_left, H)
    came[4].wait_recv()
    left_t[:, pl.ds(R, R)] = scaled_t(1, own_left, H)
    came[5].wait_recv()

    def left_step(step, carry):
        here = pl.ds(pl.multiple_of(step * Q, Q), Q)
        total[:, here] = gram(left_t[...], rows[:, here])
        return carry

    lax.fori_loop(0, B // Q, left_step, 0)

    def cross_step(step, carry):
        here = pl.ds(pl.multiple_of(step * Q, Q), Q)
        there = pl.ds(pl.multiple_of(B + step * Q, Q), Q)
        cross_ref[:, here] = gram(left_t[...], rows[:, there]).astype(BF16)
        return carry

    def handed(which):
        return pltpu.make_async_remote_copy(
            src_ref=in_tiles.at[pl.ds(which * Q, Q), :],
            dst_ref=peer_tiles.at[pl.ds(which * Q, Q), :],
            send_sem=pass_send.at[which],
            recv_sem=pass_recv.at[which],
            device_id=peer,
            device_id_type=MESH,
        )

    passes = [handed(0), handed(1)]

    @pl.when(has_before)
    def _():
        links[0].wait_recv()
        passes[0].start()

    lax.fori_loop(0, B // Q, cross_step, 0)

    def columns(half, tile):
        return pl.ds(pl.multiple_of(half * H + tile * Q, Q), Q)

    def band(tile):
        return pl.ds(pl.multiple_of(tile * Q, Q), Q)

    def put(row_tile, where, value):
        diag_ref[band(row_tile), where] = (total[band(row_tile), where] + value).astype(BF16)

    @pl.when(t == 0)
    def _():
        diag_ref[...] = total[...].astype(BF16)

    @pl.when(has_before)
    def _():
        put(0, columns(q, p), in_tiles[pl.ds(0, Q), :].astype(F32))
        links[1].wait_recv()
        passes[1].start()
        put(1, columns(q, 1 - p), in_tiles[pl.ds(Q, Q), :].astype(F32))
        for tile in range(2):
            passes[tile].wait_recv()
            turned = peer_tiles[pl.ds(tile * Q, Q), :].astype(F32).T
            put(lax.rem(tile + q, 2), columns(q, tile), turned)
        links[2].wait_recv()
        square = in_tiles[pl.ds(2 * Q, Q), :].astype(F32)
        put(0, columns(p, 1), square)
        put(1, columns(p, 0), square.T)
        links[3].wait_recv()
        packed = in_tiles[pl.ds(3 * Q, Q), :].astype(F32)
        turned = packed.T
        put(0, columns(p, 0), jnp.where(upper >= lower, packed, turned))
        middle_row = in_tiles[pl.ds(4 * Q, PAD), :].astype(F32)[0:1, :]
        put(
            1,
            columns(p, 1),
            jnp.where(
                upper == lower,
                jnp.broadcast_to(middle_row, (Q, Q)),
                jnp.where(upper < lower, packed, turned),
            ),
        )
        for copy in passes:
            copy.wait_send()

    weight_copy.wait_send()
    for copy in sent:
        copy.wait_send()

    @pl.when(has_after)
    def _():
        for copy in links:
            copy.wait_send()


def body(panels, barrier, counts):
    R = panels.shape[1]
    B = panels.shape[2] // 2
    H = B // 2
    Q = H // 2
    tiles = 4 * Q + PAD
    flops = 2 * 3 * H * B * 2 * R
    diag, cross = pl.pallas_call(
        functools.partial(kernel, lax.axis_size("tm")),
        out_shape=(
            jax.ShapeDtypeStruct((H, B), BF16),
            jax.ShapeDtypeStruct((H, B), BF16),
        ),
        in_specs=[
            pl.BlockSpec(memory_space=pl.ANY),
            pl.BlockSpec(memory_space=pltpu.VMEM),
            pl.BlockSpec(memory_space=pltpu.SMEM),
        ],
        out_specs=(
            pl.BlockSpec(memory_space=pltpu.VMEM),
            pl.BlockSpec(memory_space=pltpu.VMEM),
        ),
        scratch_shapes=[
            pltpu.VMEM((2 * R, 2 * B), BF16),
            pltpu.VMEM((8, R), F32),
            pltpu.VMEM((8, R), F32),
            pltpu.VMEM((2 * R, 128), F32),
            pltpu.VMEM((H, 2 * R), BF16),
            pltpu.VMEM((H, 2 * R), BF16),
            pltpu.VMEM((H, B), F32),
            pltpu.VMEM((tiles, Q), BF16),
            pltpu.VMEM((tiles, Q), BF16),
            pltpu.VMEM((2 * Q, Q), BF16),
            pltpu.SemaphoreType.DMA((2,)),
            pltpu.SemaphoreType.DMA((7,)),
            pltpu.SemaphoreType.DMA((7,)),
            pltpu.SemaphoreType.DMA((4,)),
            pltpu.SemaphoreType.DMA((4,)),
            pltpu.SemaphoreType.DMA((2,)),
            pltpu.SemaphoreType.DMA((2,)),
        ],
        compiler_params=pltpu.CompilerParams(
            collective_id=0, has_side_effects=True, vmem_limit_bytes=48 * 1024 * 1024
        ),
        cost_estimate=pl.CostEstimate(
            flops=flops, bytes_accessed=4 * R * B * 2 + 4 * H * B, transcendentals=0
        ),
    )(panels, barrier, counts)
    return diag[None], cross[None]


def solution(mesh):
    return jax.shard_map(
        body,
        mesh=mesh,
        in_specs=(
            P(("scen", "tm"), "panel", None),
            P(("scen", "tm"), "panel"),
            P(("scen", "tm"), "panel"),
        ),
        out_specs=(P(("scen", "tm"), "panel", None), P(("scen", "tm"), "panel", None)),
        check_vma=False,
    )
```

time: 112 us -> 23.8 us (0.21)
  waiting for transfers between devices: 66.2 us -> 0 us
  Pallas kernels: 0 us -> 18.1 us
  between operations: 14.7 us -> 1.29 us
  other arithmetic: 12.2 us -> 0 us
  matrix products: 10.5 us -> 0 us
  starting transfers between devices: 3.1 us -> 0 us
    ppermute x1 -> x0, waiting for transfers between devices: 35.6 us -> none  [passed_along(): return lax.ppermute(value, axis, pairs)]
    psum x1 -> x0, waiting for transfers between devices: 30.6 us -> none  [body(): lax.psum(diag_term.astype(jnp.bfloat16), 'panel').astype(jnp.float32)]
    pallas_call x0 -> x1, Pallas kernels: none -> 18.1 us  [body(): pl.pallas_call(functools.partial(kernel, lax.axis_size('tm')), out_shape=...]
    dot_general x2 -> x0, matrix products: 10.5 us -> none  [prefix_gram(): lax.dot_general(left_part[:row_count], right_part[:row_count], (((0,), (0...]
    convert_element_type x3 -> x0, other arithmetic: 9.19 us -> none  [the longest x1 4.97 us: body(): (left_cross[:, :states] + came_right.astype(jnp.float32)).astype(jnp.bflo...]
    unnamed x2 -> x6, local copies, waits for them, and re-layouts: 0.01 us -> 4.21 us
    slice x1 -> x0, local copies, waits for them, and re-layouts: 3.91 us -> none  [body(): cross_round = left_cross[:, states:].astype(jnp.bfloat16)]
    ppermute x1 -> x0, starting transfers between devices: 3.06 us -> none  [passed_along(): return lax.ppermute(value, axis, pairs)]
  transfers between devices with their start and end apart: 2 -> 0, of which waited for: 2 -> 0; matrix products, arithmetic and copies ran while one was open for 10% -> 0% of each run, Pallas kernels for 0% -> 0%
where the time goes in v1:
time: 23.8 us; the launch traced here: 23.6 us
  Pallas kernels  18.1 us (76%)
  local copies, waits for them, and re-layouts  4.21 us (18%)
  between operations  1.29 us (5%)
    pallas_call x1, Pallas kernels, body(): pl.pallas_call(functools.partial(kernel, lax.axis_size('tm')), out_shape=...  18.1 us
    unnamed x6, local copies, waits for them, and re-layouts  4.21 us

profile of v1, /device:TPU:9, one launch (start us, length us, event | category | flops | bytes accessed | tf_op | source)
XLA Modules:
  0.0 23.6 jit_solution(7691940831533781149)
XLA Ops:
  1.3 0.0 copy-start
  1.3 1.6 %copy-done = bf16[1,512,2048]{2,1,0:T(8,128)(2,1)S(1)} copy-done((bf16[1,512,2048]{2,1,0:T(8,128)(2,1)S(1)}, bf16[1,512,2048]{2,1,0:T(8,128)(2,1)}, u32[]{:S(2)}) %copy-start) | copy-done | bytes 2097176
  2.9 0.0 copy-start.1
  2.9 0.7 %copy-done.1 = bf16[1,512]{1,0:T(2,128)(2,1)S(1)} copy-done((bf16[1,512]{1,0:T(2,128)(2,1)S(1)}, bf16[1,512]{1,0:T(2,128)(2,1)}, u32[]{:S(2)}) %copy-start.1) | copy-done | bytes 1048
  3.6 18.1 %shard_map.50 = (bf16[512,1024]{1,0:T(8,128)(2,1)S(1)}, bf16[512,1024]{1,0:T(8,128)(2,1)S(1)}) custom-call(bf16[1,512,2048]{2,1,0:T(8,128)(2,1)S(1)} %copy-done, bf16[1,512]{1,0:T(2,128)(2,1)S(1)} %copy-done.1, s32[1,1]{1,0:T(1,128)S(6)} %copy.7.counts_ref), custom_call_target="tpu_custom_call" | custom-call | flops 3221225472 | bytes 6291456 | tf_op jit(solution)/shard_map/pallas_call | solution.py:276
  21.7 1.0 %copy.8 = bf16[1,512,1024]{2,1,0:T(8,128)(2,1)} copy(bf16[1,512,1024]{2,1,0:T(8,128)(2,1)S(1)} %bitcast.3) | data formatting | bytes 2097152
  22.7 1.0 %copy.9 = bf16[1,512,1024]{2,1,0:T(8,128)(2,1)} copy(bf16[1,512,1024]{2,1,0:T(8,128)(2,1)S(1)} %bitcast.2) | data formatting | bytes 2097152
Async XLA Ops:
  1.3 1.6 %copy-start = (bf16[1,512,2048]{2,1,0:T(8,128)(2,1)S(1)}, bf16[1,512,2048]{2,1,0:T(8,128)(2,1)}, u32[]{:S(2)}) copy-start(bf16[1,512,2048]{2,1,0:T(8,128)(2,1)} %panels_ref.1) | copy-start | bytes 6291460
  2.9 0.7 %copy-start.1 = (bf16[1,512]{1,0:T(2,128)(2,1)S(1)}, bf16[1,512]{1,0:T(2,128)(2,1)}, u32[]{:S(2)}) copy-start(bf16[1,512]{1,0:T(2,128)(2,1)} %barrier_ref.1) | copy-start | bytes 3076

commit v2 on v1

--- a/solution.py
+++ b/solution.py
@@ -8,10 +8,12 @@
 from jax.sharding import PartitionSpec as P
 
 PR = 64
+VMEM_BYTES = 50 * 1024 * 1024
 MESH = pl.DeviceIdType.MESH
 F32 = jnp.float32
 BF16 = jnp.bfloat16
 PAD = 16
+PIECES = 4
 
 
 def gram(left, right):
@@ -26,6 +28,8 @@
     diag_ref,
     cross_ref,
     rows,
+    diagonal_row,
+    count,
     weight_row,
     weight_peer,
     weight_col,
@@ -60,6 +64,10 @@
     local_left = pltpu.make_async_copy(
         panels_ref.at[0, :, pl.ds(0, B)], rows.at[pl.ds(0, R), pl.ds(0, B)], local_sem.at[1]
     )
+    diagonal_copy = pltpu.make_async_copy(barrier_ref, diagonal_row, local_sem.at[2])
+    count_copy = pltpu.make_async_copy(counts_ref, count, local_sem.at[3])
+    count_copy.start()
+    diagonal_copy.start()
     local_right.start()
     local_left.start()
 
@@ -75,8 +83,10 @@
         pl.semaphore_signal(entry, inc=1, device_id=after, device_id_type=MESH)
 
     spot = lax.broadcasted_iota(jnp.int32, (8, R), 1)
-    diagonal = jnp.broadcast_to(barrier_ref[...].astype(F32), (8, R))
-    weight_row[...] = jnp.where(spot < counts_ref[0, 0] * PR, diagonal, 0.0)
+    count_copy.wait()
+    diagonal_copy.wait()
+    diagonal = jnp.broadcast_to(diagonal_row[...].astype(F32), (8, R))
+    weight_row[...] = jnp.where(spot < count[0, 0] * PR, diagonal, 0.0)
 
     def right_tile(half, tile):
         return pl.ds(pl.multiple_of(B + half * H + tile * Q, Q), Q)
@@ -266,6 +276,25 @@
             copy.wait_send()
 
 
+def write_out(diag_ref, cross_ref, diag_out, cross_out, sems):
+    length = diag_ref.shape[0] // PIECES
+    copies = []
+    for piece in range(PIECES):
+        here = pl.ds(piece * length, length)
+        copies.append(
+            pltpu.make_async_copy(diag_ref.at[here], diag_out.at[0, here], sems.at[2 * piece])
+        )
+        copies.append(
+            pltpu.make_async_copy(
+                cross_ref.at[here], cross_out.at[0, here], sems.at[2 * piece + 1]
+            )
+        )
+    for copy in copies:
+        copy.start()
+    for copy in copies:
+        copy.wait()
+
+
 def body(panels, barrier, counts):
     R = panels.shape[1]
     B = panels.shape[2] // 2
@@ -280,9 +309,9 @@
             jax.ShapeDtypeStruct((H, B), BF16),
         ),
         in_specs=[
-            pl.BlockSpec(memory_space=pl.ANY),
-            pl.BlockSpec(memory_space=pltpu.VMEM),
-            pl.BlockSpec(memory_space=pltpu.SMEM),
+            pl.BlockSpec(memory_space=pltpu.HBM),
+            pl.BlockSpec(memory_space=pltpu.HBM),
+            pl.BlockSpec(memory_space=pltpu.HBM),
         ],
         out_specs=(
             pl.BlockSpec(memory_space=pltpu.VMEM),
@@ -290,6 +319,8 @@
         ),
         scratch_shapes=[
             pltpu.VMEM((2 * R, 2 * B), BF16),
+            pltpu.VMEM((1, R), BF16),
+            pltpu.SMEM((1, 1), jnp.int32),
             pltpu.VMEM((8, R), F32),
             pltpu.VMEM((8, R), F32),
             pltpu.VMEM((2 * R, 128), F32),
@@ -299,7 +330,7 @@
             pltpu.VMEM((tiles, Q), BF16),
             pltpu.VMEM((tiles, Q), BF16),
             pltpu.VMEM((2 * Q, Q), BF16),
-            pltpu.SemaphoreType.DMA((2,)),
+            pltpu.SemaphoreType.DMA((4,)),
             pltpu.SemaphoreType.DMA((7,)),
             pltpu.SemaphoreType.DMA((7,)),
             pltpu.SemaphoreType.DMA((4,)),
@@ -308,13 +339,24 @@
             pltpu.SemaphoreType.DMA((2,)),
         ],
         compiler_params=pltpu.CompilerParams(
-            collective_id=0, has_side_effects=True, vmem_limit_bytes=48 * 1024 * 1024
+            collective_id=0, has_side_effects=True, vmem_limit_bytes=VMEM_BYTES
         ),
         cost_estimate=pl.CostEstimate(
             flops=flops, bytes_accessed=4 * R * B * 2 + 4 * H * B, transcendentals=0
         ),
     )(panels, barrier, counts)
-    return diag[None], cross[None]
+    return tuple(
+        pl.pallas_call(
+            write_out,
+            out_shape=(
+                jax.ShapeDtypeStruct((1, H, B), BF16),
+                jax.ShapeDtypeStruct((1, H, B), BF16),
+            ),
+            in_specs=[pl.BlockSpec(memory_space=pltpu.VMEM)] * 2,
+            out_specs=(pl.BlockSpec(memory_space=pl.ANY), pl.BlockSpec(memory_space=pl.ANY)),
+            scratch_shapes=[pltpu.SemaphoreType.DMA((2 * PIECES,))],
+        )(diag, cross)
+    )
 
 
 def solution(mesh):

time: 23.8 us -> 24.9 us (1.046)
  Pallas kernels: 18.1 us -> 20.8 us
  local copies, waits for them, and re-layouts: 4.21 us -> 2.65 us
    pallas_call x0 -> x1, Pallas kernels: none -> 2.91 us  [body(): pl.pallas_call(write_out, out_shape=(jax.ShapeDtypeStruct((1, H, B), BF16...]
    unnamed x6, local copies, waits for them, and re-layouts: 4.21 us -> 2.65 us
    pallas_call x1, Pallas kernels: 18.1 us -> 17.9 us  [body(): pl.pallas_call(functools.partial(kernel, lax.axis_size('tm')), out_shape=...]
where the time goes in v2:
time: 24.9 us; the launch traced here: 24.7 us
  Pallas kernels  20.8 us (84%)
  local copies, waits for them, and re-layouts  2.65 us (11%)
  between operations  1.3 us (5%)
    pallas_call x1, Pallas kernels, body(): pl.pallas_call(functools.partial(kernel, lax.axis_size('tm')), out_shape=...  17.9 us
    pallas_call x1, Pallas kernels, body(): pl.pallas_call(write_out, out_shape=(jax.ShapeDtypeStruct((1, H, B), BF16...  2.91 us
    unnamed x6, local copies, waits for them, and re-layouts  2.65 us

profile of v2, /device:TPU:9, one launch (start us, length us, event | category | flops | bytes accessed | tf_op | source)
XLA Modules:
  0.0 24.7 jit_solution(1913596202228847687)
XLA Ops:
  1.3 0.0 copy-start.2
  1.3 0.7 %copy-done.2 = bf16[1,512]{1,0:T(2,128)(2,1)S(1)} copy-done((bf16[1,512]{1,0:T(2,128)(2,1)S(1)}, bf16[1,512]{1,0:T(2,128)(2,1)}, u32[]{:S(2)}) %copy-start.2) | copy-done | bytes 1048
  2.0 17.9 %shard_map.50 = (bf16[512,1024]{1,0:T(8,128)(2,1)S(1)}, bf16[512,1024]{1,0:T(8,128)(2,1)S(1)}) custom-call(bf16[1,512,2048]{2,1,0:T(8,128)(2,1)} %panels_ref.1, bf16[1,512]{1,0:T(2,128)(2,1)S(1)} %copy-done.2, s32[1,1]{1,0:T(1,128)S(6)} %copy.5.counts_ref), custom_call_target="tpu_custom_call" | custom-call | flops 3221225472 | bytes 6291456 | tf_op jit(solution)/shard_map/pallas_call | solution.py:305
  19.8 0.0 copy-start
  19.8 1.0 %copy-done = bf16[512,1024]{1,0:T(8,128)(2,1)} copy-done((bf16[512,1024]{1,0:T(8,128)(2,1)}, bf16[512,1024]{1,0:T(8,128)(2,1)S(1)}, u32[]{:S(2)}) %copy-start) | copy-done | bytes 1048600
  20.8 0.0 copy-start.1
  20.8 1.0 %copy-done.1 = bf16[512,1024]{1,0:T(8,128)(2,1)} copy-done((bf16[512,1024]{1,0:T(8,128)(2,1)}, bf16[512,1024]{1,0:T(8,128)(2,1)S(1)}, u32[]{:S(2)}) %copy-start.1) | copy-done | bytes 1048600
  21.8 2.9 %shard_map.51 = (bf16[1,512,1024]{2,1,0:T(8,128)(2,1)}, bf16[1,512,1024]{2,1,0:T(8,128)(2,1)}) custom-call(bf16[512,1024]{1,0:T(8,128)(2,1)} %copy-done, bf16[512,1024]{1,0:T(8,128)(2,1)} %copy-done.1), custom_call_target="tpu_custom_call" | custom-call | tf_op jit(solution)/shard_map/pallas_call | solution.py:349
Async XLA Ops:
  1.3 0.7 %copy-start.2 = (bf16[1,512]{1,0:T(2,128)(2,1)S(1)}, bf16[1,512]{1,0:T(2,128)(2,1)}, u32[]{:S(2)}) copy-start(bf16[1,512]{1,0:T(2,128)(2,1)} %barrier_ref.1) | copy-start | bytes 3076
  19.8 1.0 %copy-start = (bf16[512,1024]{1,0:T(8,128)(2,1)}, bf16[512,1024]{1,0:T(8,128)(2,1)S(1)}, u32[]{:S(2)}) copy-start(bf16[512,1024]{1,0:T(8,128)(2,1)S(1)} %get-tuple-element.4.diag_ref) | copy-start | bytes 3145732
  20.8 1.0 %copy-start.1 = (bf16[512,1024]{1,0:T(8,128)(2,1)}, bf16[512,1024]{1,0:T(8,128)(2,1)S(1)}, u32[]{:S(2)}) copy-start(bf16[512,1024]{1,0:T(8,128)(2,1)S(1)} %get-tuple-element.5.cross_ref) | copy-start | bytes 3145732

commit v3 on v1

--- a/solution.py
+++ b/solution.py
@@ -8,6 +8,7 @@
 from jax.sharding import PartitionSpec as P
 
 PR = 64
+VMEM_BYTES = 48 * 1024 * 1024
 MESH = pl.DeviceIdType.MESH
 F32 = jnp.float32
 BF16 = jnp.bfloat16
@@ -26,6 +27,7 @@
     diag_ref,
     cross_ref,
     rows,
+    diagonal_row,
     weight_row,
     weight_peer,
     weight_col,
@@ -47,6 +49,7 @@
     B = panels_ref.shape[2] // 2
     H = B // 2
     Q = H // 2
+    E = Q // 2
     s, t, p = lax.axis_index("scen"), lax.axis_index("tm"), lax.axis_index("panel")
     q = 1 - p
     peer = (s, t, q)
@@ -60,6 +63,8 @@
     local_left = pltpu.make_async_copy(
         panels_ref.at[0, :, pl.ds(0, B)], rows.at[pl.ds(0, R), pl.ds(0, B)], local_sem.at[1]
     )
+    diagonal_copy = pltpu.make_async_copy(barrier_ref, diagonal_row, local_sem.at[2])
+    diagonal_copy.start()
     local_right.start()
     local_left.start()
 
@@ -75,7 +80,8 @@
         pl.semaphore_signal(entry, inc=1, device_id=after, device_id_type=MESH)
 
     spot = lax.broadcasted_iota(jnp.int32, (8, R), 1)
-    diagonal = jnp.broadcast_to(barrier_ref[...].astype(F32), (8, R))
+    diagonal_copy.wait()
+    diagonal = jnp.broadcast_to(diagonal_row[...].astype(F32), (8, R))
     weight_row[...] = jnp.where(spot < counts_ref[0, 0] * PR, diagonal, 0.0)
 
     def right_tile(half, tile):
@@ -143,7 +149,13 @@
             device_id_type=MESH,
         )
 
-    links = [link(0, Q, 0), link(Q, Q, 1), link(2 * Q, Q, 2), link(3 * Q, Q + PAD, 3)]
+    links = [
+        link(0, Q, 0),
+        link(Q, Q, 1),
+        link(2 * Q, Q + PAD, 2),
+        link(3 * Q + PAD, E, 3),
+        link(3 * Q + PAD + E, E, 4),
+    ]
 
     def send_on(which):
         @pl.when(has_after)
@@ -162,16 +174,17 @@
             right_t[pl.ds(tile * Q, Q), :], rows[:, right_tile(q, other)]
         ).astype(BF16)
         send_on(tile)
-    out_tiles[pl.ds(2 * Q, Q), :] = gram(
-        right_t[pl.ds(0, Q), :], rows[:, right_tile(p, 1)]
-    ).astype(BF16)
-    send_on(2)
     first = gram(right_t[pl.ds(0, Q), :], rows[:, right_tile(p, 0)])
     second = gram(right_t[pl.ds(Q, Q), :], rows[:, right_tile(p, 1)])
-    out_tiles[pl.ds(3 * Q, Q), :] = jnp.where(upper >= lower, first, second).astype(BF16)
+    out_tiles[pl.ds(2 * Q, Q), :] = jnp.where(upper >= lower, first, second).astype(BF16)
     middle = jnp.sum(jnp.where(upper == lower, second, 0.0), axis=0, keepdims=True)
-    out_tiles[pl.ds(4 * Q, PAD), :] = jnp.broadcast_to(middle, (PAD, Q)).astype(BF16)
-    send_on(3)
+    out_tiles[pl.ds(3 * Q, PAD), :] = jnp.broadcast_to(middle, (PAD, Q)).astype(BF16)
+    send_on(2)
+    for part in range(2):
+        out_tiles[pl.ds(3 * Q + PAD + part * E, E), :] = gram(
+            right_t[pl.ds(part * E, E), :], rows[:, right_tile(p, 1)]
+        ).astype(BF16)
+        send_on(3 + part)
 
     own_left = pl.ds(pl.multiple_of(p * H, H), H)
     local_left.wait()
@@ -236,14 +249,10 @@
             turned = peer_tiles[pl.ds(tile * Q, Q), :].astype(F32).T
             put(lax.rem(tile + q, 2), columns(q, tile), turned)
         links[2].wait_recv()
-        square = in_tiles[pl.ds(2 * Q, Q), :].astype(F32)
-        put(0, columns(p, 1), square)
-        put(1, columns(p, 0), square.T)
-        links[3].wait_recv()
-        packed = in_tiles[pl.ds(3 * Q, Q), :].astype(F32)
+        packed = in_tiles[pl.ds(2 * Q, Q), :].astype(F32)
         turned = packed.T
         put(0, columns(p, 0), jnp.where(upper >= lower, packed, turned))
-        middle_row = in_tiles[pl.ds(4 * Q, PAD), :].astype(F32)[0:1, :]
+        middle_row = in_tiles[pl.ds(3 * Q, PAD), :].astype(F32)[0:1, :]
         put(
             1,
             columns(p, 1),
@@ -253,6 +262,13 @@
                 jnp.where(upper < lower, packed, turned),
             ),
         )
+        for part in range(2):
+            links[3 + part].wait_recv()
+            piece = in_tiles[pl.ds(3 * Q + PAD + part * E, E), :].astype(F32)
+            across = pl.ds(part * E, E)
+            diag_ref[across, columns(p, 1)] = (total[across, columns(p, 1)] + piece).astype(BF16)
+            down = pl.ds(pl.multiple_of(p * H + part * E, E), E)
+            diag_ref[pl.ds(Q, Q), down] = (total[pl.ds(Q, Q), down] + piece.T).astype(BF16)
         for copy in passes:
             copy.wait_send()
 
@@ -264,6 +280,10 @@
     def _():
         for copy in links:
             copy.wait_send()
+
+
+def in_hbm(array):
+    return pltpu.with_memory_space_constraint(array, pltpu.HBM)
 
 
 def body(panels, barrier, counts):
@@ -280,8 +300,8 @@
             jax.ShapeDtypeStruct((H, B), BF16),
         ),
         in_specs=[
-            pl.BlockSpec(memory_space=pl.ANY),
-            pl.BlockSpec(memory_space=pltpu.VMEM),
+            pl.BlockSpec(memory_space=pltpu.HBM),
+            pl.BlockSpec(memory_space=pltpu.HBM),
             pl.BlockSpec(memory_space=pltpu.SMEM),
         ],
         out_specs=(
@@ -290,6 +310,7 @@
         ),
         scratch_shapes=[
             pltpu.VMEM((2 * R, 2 * B), BF16),
+            pltpu.VMEM((1, R), BF16),
             pltpu.VMEM((8, R), F32),
             pltpu.VMEM((8, R), F32),
             pltpu.VMEM((2 * R, 128), F32),
@@ -299,21 +320,21 @@
             pltpu.VMEM((tiles, Q), BF16),
             pltpu.VMEM((tiles, Q), BF16),
             pltpu.VMEM((2 * Q, Q), BF16),
-            pltpu.SemaphoreType.DMA((2,)),
+            pltpu.SemaphoreType.DMA((3,)),
             pltpu.SemaphoreType.DMA((7,)),
             pltpu.SemaphoreType.DMA((7,)),
-            pltpu.SemaphoreType.DMA((4,)),
-            pltpu.SemaphoreType.DMA((4,)),
+            pltpu.SemaphoreType.DMA((5,)),
+            pltpu.SemaphoreType.DMA((5,)),
             pltpu.SemaphoreType.DMA((2,)),
             pltpu.SemaphoreType.DMA((2,)),
         ],
         compiler_params=pltpu.CompilerParams(
-            collective_id=0, has_side_effects=True, vmem_limit_bytes=48 * 1024 * 1024
+            collective_id=0, has_side_effects=True, vmem_limit_bytes=VMEM_BYTES
         ),
         cost_estimate=pl.CostEstimate(
             flops=flops, bytes_accessed=4 * R * B * 2 + 4 * H * B, transcendentals=0
         ),
-    )(panels, barrier, counts)
+    )(in_hbm(panels), in_hbm(barrier), counts)
     return diag[None], cross[None]
 
 

time: 23.8 us -> 21.4 us (0.90)
  local copies, waits for them, and re-layouts: 4.21 us -> 1.94 us
    unnamed x6 -> x2, local copies, waits for them, and re-layouts: 4.21 us -> 1.94 us
where the time goes in v3:
time: 21.4 us; the launch traced here: 21.2 us
  Pallas kernels  18 us (84%)
  local copies, waits for them, and re-layouts  1.94 us (9%)
  between operations  1.28 us (6%)
    pallas_call x1, Pallas kernels, body(): pl.pallas_call(functools.partial(kernel, lax.axis_size('tm')), out_shape=...  18 us
    unnamed x2, local copies, waits for them, and re-layouts  1.94 us

profile of v3, /device:TPU:9, one launch (start us, length us, event | category | flops | bytes accessed | tf_op | source)
XLA Modules:
  0.0 21.2 jit_solution(745440517284826973)
XLA Ops:
  1.3 18.0 %shard_map.50 = (bf16[512,1024]{1,0:T(8,128)(2,1)S(1)}, bf16[512,1024]{1,0:T(8,128)(2,1)S(1)}) custom-call(bf16[1,512,2048]{2,1,0:T(8,128)(2,1)} %panels_ref.1, bf16[1,512]{1,0:T(2,128)(2,1)} %barrier_ref.1, s32[1,1]{1,0:T(1,128)S(6)} %copy.7.counts_ref), custom_call_target="tpu_custom_call" | custom-call | flops 3221225472 | bytes 6291456 | tf_op jit(solution)/shard_map/pallas_call | solution.py:296
  19.2 1.0 %copy.8 = bf16[1,512,1024]{2,1,0:T(8,128)(2,1)} copy(bf16[1,512,1024]{2,1,0:T(8,128)(2,1)S(1)} %bitcast.3) | data formatting | bytes 2097152
  20.2 1.0 %copy.9 = bf16[1,512,1024]{2,1,0:T(8,128)(2,1)} copy(bf16[1,512,1024]{2,1,0:T(8,128)(2,1)S(1)} %bitcast.2) | data formatting | bytes 2097152

commit v4 on v3

--- a/solution.py
+++ b/solution.py
@@ -34,12 +34,16 @@
     right_t,
     left_t,
     total,
+    part_out,
+    part_in,
     out_tiles,
     in_tiles,
     peer_tiles,
     local_sem,
     peer_send,
     peer_recv,
+    part_send,
+    part_recv,
     link_send,
     link_recv,
     pass_send,
@@ -57,15 +61,25 @@
     before = (s, lax.rem(t + blocks - 1, blocks), p)
     has_before, has_after = t > 0, t < blocks - 1
 
-    local_right = pltpu.make_async_copy(
-        panels_ref.at[0, :, pl.ds(B, B)], rows.at[pl.ds(0, R), pl.ds(B, B)], local_sem.at[0]
-    )
-    local_left = pltpu.make_async_copy(
-        panels_ref.at[0, :, pl.ds(0, B)], rows.at[pl.ds(0, R), pl.ds(0, B)], local_sem.at[1]
-    )
-    diagonal_copy = pltpu.make_async_copy(barrier_ref, diagonal_row, local_sem.at[2])
+    def right_tile(half, tile):
+        return pl.ds(pl.multiple_of(B + half * H + tile * Q, Q), Q)
+
+    def local(columns, which):
+        return pltpu.make_async_copy(
+            panels_ref.at[0, :, columns], rows.at[pl.ds(0, R), columns], local_sem.at[which]
+        )
+
+    diagonal_copy = pltpu.make_async_copy(barrier_ref, diagonal_row, local_sem.at[5])
     diagonal_copy.start()
-    local_right.start()
+    local_right = [
+        local(right_tile(q, 0), 0),
+        local(right_tile(p, q), 1),
+        local(right_tile(q, 1), 2),
+        local(right_tile(p, p), 3),
+    ]
+    local_left = local(pl.ds(0, B), 4)
+    for copy in local_right:
+        copy.start()
     local_left.start()
 
     entry = pltpu.get_barrier_semaphore()
@@ -83,9 +97,6 @@
     diagonal_copy.wait()
     diagonal = jnp.broadcast_to(diagonal_row[...].astype(F32), (8, R))
     weight_row[...] = jnp.where(spot < counts_ref[0, 0] * PR, diagonal, 0.0)
-
-    def right_tile(half, tile):
-        return pl.ds(pl.multiple_of(B + half * H + tile * Q, Q), Q)
 
     def to_peer(columns, which):
         return pltpu.make_async_remote_copy(
@@ -98,31 +109,24 @@
         )
 
     def exchange(dest):
-        rest = 1 - dest
         return [
-            to_peer(right_tile(dest, 0), 0),
-            to_peer(right_tile(rest, dest), 1),
-            to_peer(right_tile(dest, 1), 2),
-            to_peer(right_tile(rest, 1 - dest), 3),
-            to_peer(pl.ds(pl.multiple_of(dest * H, H), H), 4),
-            to_peer(pl.ds(pl.multiple_of(rest * H, H), H), 5),
+            to_peer(pl.ds(pl.multiple_of(dest * H, H), H), 0),
+            to_peer(pl.ds(pl.multiple_of((1 - dest) * H, H), H), 1),
+            to_peer(pl.ds(B, H), 2),
+            to_peer(pl.ds(B + H, H), 3),
         ]
+
+    sent = exchange(q)
+    came = exchange(p)
 
     weight_copy = pltpu.make_async_remote_copy(
         src_ref=weight_row,
         dst_ref=weight_peer,
-        send_sem=peer_send.at[6],
-        recv_sem=peer_recv.at[6],
+        send_sem=peer_send.at[4],
+        recv_sem=peer_recv.at[4],
         device_id=peer,
         device_id_type=MESH,
     )
-    pl.semaphore_wait(entry, 1 + has_before.astype(jnp.int32) + has_after.astype(jnp.int32))
-    weight_copy.start()
-    sent = exchange(q)
-    came = exchange(p)
-    for copy in sent:
-        copy.start()
-
     def spread(row):
         return jnp.broadcast_to(row[0:1, :], (128, R)).T
 
@@ -131,13 +135,6 @@
         plain = rows[pl.ds(group * R, R), columns].astype(F32)
         weight = jnp.concatenate([weight] * (width // 128), axis=1)
         return (plain * weight).astype(BF16).T
-
-    weight_col[pl.ds(0, R), :] = spread(weight_row[...])
-    local_right.wait()
-    for tile in range(2):
-        right_t[pl.ds(tile * Q, Q), pl.ds(0, R)] = scaled_t(0, right_tile(p, tile), Q)
-    weight_copy.wait_recv()
-    weight_col[pl.ds(R, R), :] = spread(weight_peer[...])
 
     def link(first, length, which):
         return pltpu.make_async_remote_copy(
@@ -165,33 +162,104 @@
     lower = lax.broadcasted_iota(jnp.int32, (Q, Q), 0)
     upper = lax.broadcasted_iota(jnp.int32, (Q, Q), 1)
 
-    for tile in range(2):
-        came[2 * tile].wait_recv()
-        right_t[pl.ds(tile * Q, Q), pl.ds(R, R)] = scaled_t(1, right_tile(p, tile), Q)
-        came[2 * tile + 1].wait_recv()
-        other = lax.rem(tile + p, 2)
-        out_tiles[pl.ds(tile * Q, Q), :] = gram(
-            right_t[pl.ds(tile * Q, Q), :], rows[:, right_tile(q, other)]
-        ).astype(BF16)
-        send_on(tile)
-    first = gram(right_t[pl.ds(0, Q), :], rows[:, right_tile(p, 0)])
-    second = gram(right_t[pl.ds(Q, Q), :], rows[:, right_tile(p, 1)])
-    out_tiles[pl.ds(2 * Q, Q), :] = jnp.where(upper >= lower, first, second).astype(BF16)
-    middle = jnp.sum(jnp.where(upper == lower, second, 0.0), axis=0, keepdims=True)
-    out_tiles[pl.ds(3 * Q, PAD), :] = jnp.broadcast_to(middle, (PAD, Q)).astype(BF16)
+    def part(first, length, which):
+        return pltpu.make_async_remote_copy(
+            src_ref=part_out.at[pl.ds(first, length), :],
+            dst_ref=part_in.at[pl.ds(first, length), :],
+            send_sem=part_send.at[which],
+            recv_sem=part_recv.at[which],
+            device_id=peer,
+            device_id_type=MESH,
+        )
+
+    parts = [part(0, Q, 0), part(Q, Q, 1), part(2 * Q, Q + PAD, 2), part(3 * Q + PAD, Q, 3)]
+
+    def turn(dest, tile):
+        half = q if dest else p
+        right_t[pl.ds((2 - 2 * dest + tile) * Q, Q), :] = scaled_t(0, right_tile(half, tile), Q)
+
+    def side(dest, tile):
+        return right_t[pl.ds((2 - 2 * dest + tile) * Q, Q), :]
+
+    def own(columns):
+        return rows[pl.ds(0, R), columns]
+
+    def across_tile(dest, tile):
+        home, away = (q, p) if dest else (p, q)
+        return gram(side(dest, tile), own(right_tile(away, lax.rem(tile + home, 2))))
+
+    def packed_tile(dest):
+        home = q if dest else p
+        first = gram(side(dest, 0), own(right_tile(home, 0)))
+        second = gram(side(dest, 1), own(right_tile(home, 1)))
+        middle = jnp.sum(jnp.where(upper == lower, second, 0.0), axis=0, keepdims=True)
+        return jnp.where(upper >= lower, first, second), jnp.broadcast_to(middle, (PAD, Q))
+
+    def square_tile(dest):
+        home = q if dest else p
+        return gram(side(dest, 0), own(right_tile(home, 1)))
+
+    weight_col[pl.ds(0, R), :] = spread(weight_row[...])
+    local_right[0].wait()
+    turn(1, 0)
+    local_right[1].wait()
+    part_out[pl.ds(0, Q), :] = across_tile(1, 0).astype(BF16)
+    pl.semaphore_wait(entry, 1 + has_before.astype(jnp.int32) + has_after.astype(jnp.int32))
+    parts[0].start()
+    weight_copy.start()
+    local_right[2].wait()
+    local_right[3].wait()
+    turn(1, 1)
+    part_out[pl.ds(Q, Q), :] = across_tile(1, 1).astype(BF16)
+    parts[1].start()
+    sent[0].start()
+    sent[1].start()
+    turn(0, 0)
+    mine = across_tile(0, 0)
+    parts[0].wait_recv()
+    out_tiles[pl.ds(0, Q), :] = (mine + part_in[pl.ds(0, Q), :].astype(F32)).astype(BF16)
+    send_on(0)
+
+    packed, middle = packed_tile(1)
+    part_out[pl.ds(2 * Q, Q), :] = packed.astype(BF16)
+    part_out[pl.ds(3 * Q, PAD), :] = middle.astype(BF16)
+    parts[2].start()
+    part_out[pl.ds(3 * Q + PAD, Q), :] = square_tile(1).astype(BF16)
+    parts[3].start()
+    sent[2].start()
+    sent[3].start()
+
+    turn(0, 1)
+    mine = across_tile(0, 1)
+    parts[1].wait_recv()
+    out_tiles[pl.ds(Q, Q), :] = (mine + part_in[pl.ds(Q, Q), :].astype(F32)).astype(BF16)
+    send_on(1)
+
+    packed, middle = packed_tile(0)
+    parts[2].wait_recv()
+    out_tiles[pl.ds(2 * Q, Q), :] = (
+        packed + part_in[pl.ds(2 * Q, Q), :].astype(F32)
+    ).astype(BF16)
+    out_tiles[pl.ds(3 * Q, PAD), :] = (
+        middle + part_in[pl.ds(3 * Q, PAD), :].astype(F32)
+    ).astype(BF16)
     send_on(2)
-    for part in range(2):
-        out_tiles[pl.ds(3 * Q + PAD + part * E, E), :] = gram(
-            right_t[pl.ds(part * E, E), :], rows[:, right_tile(p, 1)]
-        ).astype(BF16)
-        send_on(3 + part)
-
+    mine = square_tile(0)
+    parts[3].wait_recv()
+    out_tiles[pl.ds(3 * Q + PAD, Q), :] = (
+        mine + part_in[pl.ds(3 * Q + PAD, Q), :].astype(F32)
+    ).astype(BF16)
+    send_on(3)
+    send_on(4)
+
+    weight_copy.wait_recv()
+    weight_col[pl.ds(R, R), :] = spread(weight_peer[...])
     own_left = pl.ds(pl.multiple_of(p * H, H), H)
     local_left.wait()
     left_t[:, pl.ds(0, R)] = scaled_t(0, own_left, H)
-    came[4].wait_recv()
+    came[0].wait_recv()
     left_t[:, pl.ds(R, R)] = scaled_t(1, own_left, H)
-    came[5].wait_recv()
+    came[1].wait_recv()
 
     def left_step(step, carry):
         here = pl.ds(pl.multiple_of(step * Q, Q), Q)
@@ -223,6 +291,8 @@
         links[0].wait_recv()
         passes[0].start()
 
+    came[2].wait_recv()
+    came[3].wait_recv()
     lax.fori_loop(0, B // Q, cross_step, 0)
 
     def columns(half, tile):
@@ -273,7 +343,7 @@
             copy.wait_send()
 
     weight_copy.wait_send()
-    for copy in sent:
+    for copy in sent + parts:
         copy.wait_send()
 
     @pl.when(has_after)
@@ -314,15 +384,19 @@
             pltpu.VMEM((8, R), F32),
             pltpu.VMEM((8, R), F32),
             pltpu.VMEM((2 * R, 128), F32),
-            pltpu.VMEM((H, 2 * R), BF16),
+            pltpu.VMEM((B, R), BF16),
             pltpu.VMEM((H, 2 * R), BF16),
             pltpu.VMEM((H, B), F32),
             pltpu.VMEM((tiles, Q), BF16),
             pltpu.VMEM((tiles, Q), BF16),
+            pltpu.VMEM((tiles, Q), BF16),
+            pltpu.VMEM((tiles, Q), BF16),
             pltpu.VMEM((2 * Q, Q), BF16),
-            pltpu.SemaphoreType.DMA((3,)),
-            pltpu.SemaphoreType.DMA((7,)),
-            pltpu.SemaphoreType.DMA((7,)),
+            pltpu.SemaphoreType.DMA((6,)),
+            pltpu.SemaphoreType.DMA((5,)),
+            pltpu.SemaphoreType.DMA((5,)),
+            pltpu.SemaphoreType.DMA((4,)),
+            pltpu.SemaphoreType.DMA((4,)),
             pltpu.SemaphoreType.DMA((5,)),
             pltpu.SemaphoreType.DMA((5,)),
             pltpu.SemaphoreType.DMA((2,)),

time: 21.4 us -> 20.7 us (0.967)
  Pallas kernels: 18 us -> 17.3 us
    pallas_call x1, Pallas kernels: 18 us -> 17.3 us  [body(): pl.pallas_call(functools.partial(kernel, lax.axis_size('tm')), out_shape=...]
where the time goes in v4:
time: 20.7 us; the launch traced here: 20.5 us
  Pallas kernels  17.3 us (84%)
  local copies, waits for them, and re-layouts  1.94 us (9%)
  between operations  1.28 us (6%)
    pallas_call x1, Pallas kernels, body(): pl.pallas_call(functools.partial(kernel, lax.axis_size('tm')), out_shape=...  17.3 us
    unnamed x2, local copies, waits for them, and re-layouts  1.94 us

profile of v4, /device:TPU:9, one launch (start us, length us, event | category | flops | bytes accessed | tf_op | source)
XLA Modules:
  0.0 20.5 jit_solution(10767280260498668583)
XLA Ops:
  1.3 17.3 %shard_map.50 = (bf16[512,1024]{1,0:T(8,128)(2,1)S(1)}, bf16[512,1024]{1,0:T(8,128)(2,1)S(1)}) custom-call(bf16[1,512,2048]{2,1,0:T(8,128)(2,1)} %panels_ref.1, bf16[1,512]{1,0:T(2,128)(2,1)} %barrier_ref.1, s32[1,1]{1,0:T(1,128)S(6)} %copy.7.counts_ref), custom_call_target="tpu_custom_call" | custom-call | flops 3221225472 | bytes 6291456 | tf_op jit(solution)/shard_map/pallas_call | solution.py:366
  18.6 1.0 %copy.8 = bf16[1,512,1024]{2,1,0:T(8,128)(2,1)} copy(bf16[1,512,1024]{2,1,0:T(8,128)(2,1)S(1)} %bitcast.3) | data formatting | bytes 2097152
  19.6 1.0 %copy.9 = bf16[1,512,1024]{2,1,0:T(8,128)(2,1)} copy(bf16[1,512,1024]{2,1,0:T(8,128)(2,1)S(1)} %bitcast.2) | data formatting | bytes 2097152

commit v5 on v4

--- a/solution.py
+++ b/solution.py
@@ -147,11 +147,12 @@
         )
 
     links = [
-        link(0, Q, 0),
+        link(0, E, 0),
         link(Q, Q, 1),
         link(2 * Q, Q + PAD, 2),
         link(3 * Q + PAD, E, 3),
         link(3 * Q + PAD + E, E, 4),
+        link(E, E, 5),
     ]
 
     def send_on(which):
@@ -172,7 +173,13 @@
             device_id_type=MESH,
         )
 
-    parts = [part(0, Q, 0), part(Q, Q, 1), part(2 * Q, Q + PAD, 2), part(3 * Q + PAD, Q, 3)]
+    parts = [
+        part(0, E, 0),
+        part(Q, Q, 1),
+        part(2 * Q, Q + PAD, 2),
+        part(3 * Q + PAD, Q, 3),
+        part(E, E, 4),
+    ]
 
     def turn(dest, tile):
         half = q if dest else p
@@ -206,20 +213,24 @@
     part_out[pl.ds(0, Q), :] = across_tile(1, 0).astype(BF16)
     pl.semaphore_wait(entry, 1 + has_before.astype(jnp.int32) + has_after.astype(jnp.int32))
     parts[0].start()
-    weight_copy.start()
+    parts[4].start()
     local_right[2].wait()
     local_right[3].wait()
+    turn(0, 0)
+    mine = across_tile(0, 0)
+    parts[0].wait_recv()
+    out_tiles[pl.ds(0, E), :] = (mine[:E] + part_in[pl.ds(0, E), :].astype(F32)).astype(BF16)
+    send_on(0)
+    parts[4].wait_recv()
+    out_tiles[pl.ds(E, E), :] = (mine[E:] + part_in[pl.ds(E, E), :].astype(F32)).astype(BF16)
+    send_on(5)
+
     turn(1, 1)
     part_out[pl.ds(Q, Q), :] = across_tile(1, 1).astype(BF16)
     parts[1].start()
+    weight_copy.start()
     sent[0].start()
     sent[1].start()
-    turn(0, 0)
-    mine = across_tile(0, 0)
-    parts[0].wait_recv()
-    out_tiles[pl.ds(0, Q), :] = (mine + part_in[pl.ds(0, Q), :].astype(F32)).astype(BF16)
-    send_on(0)
-
     packed, middle = packed_tile(1)
     part_out[pl.ds(2 * Q, Q), :] = packed.astype(BF16)
     part_out[pl.ds(3 * Q, PAD), :] = middle.astype(BF16)
@@ -289,6 +300,7 @@
     @pl.when(has_before)
     def _():
         links[0].wait_recv()
+        links[5].wait_recv()
         passes[0].start()
 
     came[2].wait_recv()
@@ -395,10 +407,10 @@
             pltpu.SemaphoreType.DMA((6,)),
             pltpu.SemaphoreType.DMA((5,)),
             pltpu.SemaphoreType.DMA((5,)),
-            pltpu.SemaphoreType.DMA((4,)),
-            pltpu.SemaphoreType.DMA((4,)),
             pltpu.SemaphoreType.DMA((5,)),
             pltpu.SemaphoreType.DMA((5,)),
+            pltpu.SemaphoreType.DMA((6,)),
+            pltpu.SemaphoreType.DMA((6,)),
             pltpu.SemaphoreType.DMA((2,)),
             pltpu.SemaphoreType.DMA((2,)),
         ],

time: 20.7 us -> 20.3 us (0.981)
  Pallas kernels: 17.3 us -> 16.9 us
    pallas_call x1, Pallas kernels: 17.3 us -> 16.9 us  [body(): pl.pallas_call(functools.partial(kernel, lax.axis_size('tm')), out_shape=...]
where the time goes in v5:
time: 20.3 us; the launch traced here: 20.1 us
  Pallas kernels  16.9 us (83%)
  local copies, waits for them, and re-layouts  1.94 us (10%)
  between operations  1.28 us (6%)
    pallas_call x1, Pallas kernels, body(): pl.pallas_call(functools.partial(kernel, lax.axis_size('tm')), out_shape=...  16.9 us
    unnamed x2, local copies, waits for them, and re-layouts  1.94 us

profile of v5, /device:TPU:9, one launch (start us, length us, event | category | flops | bytes accessed | tf_op | source)
XLA Modules:
  0.0 20.1 jit_solution(4287289692028326666)
XLA Ops:
  1.3 16.9 %shard_map.50 = (bf16[512,1024]{1,0:T(8,128)(2,1)S(1)}, bf16[512,1024]{1,0:T(8,128)(2,1)S(1)}) custom-call(bf16[1,512,2048]{2,1,0:T(8,128)(2,1)} %panels_ref.1, bf16[1,512]{1,0:T(2,128)(2,1)} %barrier_ref.1, s32[1,1]{1,0:T(1,128)S(6)} %copy.7.counts_ref), custom_call_target="tpu_custom_call" | custom-call | flops 3221225472 | bytes 6291456 | tf_op jit(solution)/shard_map/pallas_call | solution.py:378
  18.2 1.0 %copy.8 = bf16[1,512,1024]{2,1,0:T(8,128)(2,1)} copy(bf16[1,512,1024]{2,1,0:T(8,128)(2,1)S(1)} %bitcast.3) | data formatting | bytes 2097152
  19.2 1.0 %copy.9 = bf16[1,512,1024]{2,1,0:T(8,128)(2,1)} copy(bf16[1,512,1024]{2,1,0:T(8,128)(2,1)S(1)} %bitcast.2) | data formatting | bytes 2097152

commit v6 on v5

--- a/solution.py
+++ b/solution.py
@@ -78,9 +78,8 @@
         local(right_tile(p, p), 3),
     ]
     local_left = local(pl.ds(0, B), 4)
-    for copy in local_right:
+    for copy in local_right[:2]:
         copy.start()
-    local_left.start()
 
     entry = pltpu.get_barrier_semaphore()
     pl.semaphore_signal(entry, inc=1, device_id=peer, device_id_type=MESH)
@@ -210,6 +209,9 @@
     local_right[0].wait()
     turn(1, 0)
     local_right[1].wait()
+    for copy in local_right[2:]:
+        copy.start()
+    local_left.start()
     part_out[pl.ds(0, Q), :] = across_tile(1, 0).astype(BF16)
     pl.semaphore_wait(entry, 1 + has_before.astype(jnp.int32) + has_after.astype(jnp.int32))
     parts[0].start()

time: 20.3 us -> 20.4 us (level)
  no operation moved by 1% of the time
where the time goes in v6:
time: 20.4 us; the launch traced here: 20.2 us
  Pallas kernels  17 us (83%)
  local copies, waits for them, and re-layouts  1.94 us (10%)
  between operations  1.28 us (6%)
    pallas_call x1, Pallas kernels, body(): pl.pallas_call(functools.partial(kernel, lax.axis_size('tm')), out_shape=...  17 us
    unnamed x2, local copies, waits for them, and re-layouts  1.94 us

profile of v6, /device:TPU:9, one launch (start us, length us, event | category | flops | bytes accessed | tf_op | source)
XLA Modules:
  0.0 20.2 jit_solution(2072908911780677789)
XLA Ops:
  1.3 17.0 %shard_map.50 = (bf16[512,1024]{1,0:T(8,128)(2,1)S(1)}, bf16[512,1024]{1,0:T(8,128)(2,1)S(1)}) custom-call(bf16[1,512,2048]{2,1,0:T(8,128)(2,1)} %panels_ref.1, bf16[1,512]{1,0:T(2,128)(2,1)} %barrier_ref.1, s32[1,1]{1,0:T(1,128)S(6)} %copy.7.counts_ref), custom_call_target="tpu_custom_call" | custom-call | flops 3221225472 | bytes 6291456 | tf_op jit(solution)/shard_map/pallas_call | solution.py:380
  18.3 1.0 %copy.8 = bf16[1,512,1024]{2,1,0:T(8,128)(2,1)} copy(bf16[1,512,1024]{2,1,0:T(8,128)(2,1)S(1)} %bitcast.3) | data formatting | bytes 2097152
  19.2 1.0 %copy.9 = bf16[1,512,1024]{2,1,0:T(8,128)(2,1)} copy(bf16[1,512,1024]{2,1,0:T(8,128)(2,1)S(1)} %bitcast.2) | data formatting | bytes 2097152
